TPU v7x, 32 devices: a whole 2x2x4 slice. The times are simulated.
32 devices in a mesh: mirror: 2 (over y), slab: 8 (over z, x), cols: 2 (over core).
Axes of the slice: x: 2, y: 2, z: 4, core: 2. Of those that a mesh axis runs over, the one named last changes fastest.
Arguments:
- right_side: float32 [2, 1024, 8192], P('mirror', 'slab', 'cols'), parts along dimension 2, may hold values from -6 to 6
- analysis: float32 [2, 1024, 1024], P('mirror'), may hold values from -0.1875 to 0.1875
- synthesis: float32 [2, 1024, 1024], P('mirror'), may hold values from -0.1875 to 0.1875
- negated_eigen: float32 [2, 1024], P('mirror'), may hold values from 0.25 to 4
- wave_square: float32 [8192], P(('cols', 'slab')), parts along dimension 0, may hold values from 0.25 to 4
Outputs:
- solution: float32 [2, 1024, 8192], P('mirror', 'slab', 'cols'), parts along dimension 2
There are 2 independent parts, one for each index of `cols`. A program takes and returns all parts, laid end to end along the dimension named above; an argument that names none is the same for every part. Nothing has to cross between parts.
All inputs are finite; a program needn't handle non-finite values.
Results may differ from a plain program's by a relative error of at most 0.0001.
Values sent between devices are 32-bit elements; how exact they have to be, the bound alone decides.
A program may use at most 64 MiB of HBM per device.

v0:
```python
import jax
import jax.numpy as jnp
from jax import lax
from jax.sharding import PartitionSpec as P


def from_partner(value, axis, bit):
    mask = 2**bit
    pairs = [(source, source ^ mask) for source in range(lax.axis_size(axis))]
    return lax.ppermute(value, axis, pairs)


def mirror_swap(slab_piece):
    return from_partner(slab_piece, "mirror", 0)


def project(column_field, analysis, synthesis, negated_eigen, wave_square):
    coefficients = jnp.dot(
        analysis, column_field, precision=lax.Precision.HIGHEST, preferred_element_type=jnp.float32
    )
    scaled = coefficients / (negated_eigen[:, None] + wave_square[None, :])
    return -jnp.dot(
        synthesis, scaled, precision=lax.Precision.HIGHEST, preferred_element_type=jnp.float32
    )


def shards(right_side, analysis, synthesis, negated_eigen, wave_square):
    own_half = right_side[0]
    parity = lax.axis_index("mirror")
    parity_sign = (1 - 2 * parity).astype(jnp.float32)
    partner = mirror_swap(own_half)
    lower_half = jnp.where(parity == 0, own_half, partner)
    upper_half = jnp.where(parity == 0, partner, own_half)
    folded = (lower_half + parity_sign * upper_half) * 0.5
    columns = lax.all_to_all(folded, "slab", split_axis=1, concat_axis=0, tiled=True)
    solved = project(columns, analysis[0], synthesis[0], negated_eigen[0], wave_square)
    returned = lax.all_to_all(solved, "slab", split_axis=0, concat_axis=1, tiled=True)
    partner_back = mirror_swap(returned)
    even_part = jnp.where(parity == 0, returned, partner_back)
    odd_part = jnp.where(parity == 0, partner_back, returned)
    result = even_part + parity_sign * odd_part
    return result[None]


def solution(mesh):
    return jax.shard_map(
        shards,
        mesh=mesh,
        in_specs=(
            P("mirror", "slab", "cols"),
            P("mirror", None, None),
            P("mirror", None, None),
            P("mirror", None),
            P(("cols", "slab")),
        ),
        out_specs=P("mirror", "slab", "cols"),
        check_vma=False,
    )
```

profile of v0, /device:TPU:0, one launch (start us, length us, event | category | flops | bytes accessed | tf_op | source)
XLA Modules:
  0.0 230.1 jit_solution(2420291480198219773)
XLA Ops:
  0.0 1.9 copy.12
  1.9 3.0 %collective-permute-start = (f32[128,4096]{0,1:T(8,128)S(1)}, f32[128,4096]{0,1:T(8,128)}, u32[]{:S(2)}, u32[]{:S(2)}) collective-permute-start(f32[128,4096]{0,1:T(8,128)S(1)} %bitcast.33), channel_id=1, source_target_pairs={{0,16},{16,0},{1,17},{17,1},{2,18},{18,2},{3,19},{19,3},{4,20},{20... | collective-permute-start | bytes 6291464 | tf_op jit(solution)/shard_map/ppermute | solution.py:10
  4.9 45.7 %collective-permute-done = f32[128,4096]{0,1:T(8,128)} collective-permute-done((f32[128,4096]{0,1:T(8,128)S(1)}, f32[128,4096]{0,1:T(8,128)}, u32[]{:S(2)}, u32[]{:S(2)}) %collective-permute-start) | collective-permute-done | bytes 2097184 | tf_op jit(solution)/shard_map/ppermute | solution.py:10
  50.7 1.9 add_multiply_fusion
  52.6 53.4 %all_to_all.38 = f32[128,8,512]{0,2,1:T(8,128)} all-to-all(f32[128,8,512]{0,2,1:T(8,128)S(1)} %bitcast.35), channel_id=1, replica_groups=mesh['mirror'=2,'slab'=8,'cols'=2] {'slab'}, dimensions={1} | all-to-all | bytes 4194304 | tf_op jit(solution)/shard_map/all_to_all | solution.py:35
  106.0 1.9 copy.13
  107.9 0.0 copy-start
  107.9 0.0 copy-start.1
  108.0 0.0 copy-start.2
  108.0 15.6 %fusion.2 = f32[512,1024]{1,0:T(8,128)S(1)} fusion(f32[1024,512]{1,0:T(8,128)S(1)} %bitcast.32, f32[1,1024,1024]{2,1,0:T(8,128)} %param.6), kind=kOutput, calls=%fused_computation.2 | convolution fusion | flops 6442450944 | bytes 8388608 | tf_op jit(solution)/shard_map/dot_general | solution.py:18
  123.6 0.0 copy-done
  123.6 0.0 copy-done.1
  123.6 0.0 copy-done.2
  123.6 7.1 %negate_bitcast_fusion = f32[64,8,8,128]{3,2,1,0:T(8,128)S(1)} fusion(f32[1,1024,1024]{2,1,0:T(8,128)S(1)} %copy-done, f32[512,1024]{1,0:T(8,128)S(1)} %fusion.2, f32[512]{0:T(512)S(1)} %copy-done.2, f32[1024]{0:T(1024)S(1)} %bitcast.38), kind=kOutput, calls=%fused_computation.7 | convolution fusion | flops 6444023808 | bytes 8394752 | tf_op jit(solution)/shard_map/dot_general | solution.py:22
  130.7 0.1 copy.18
  130.8 51.1 %all_to_all.39 = f32[8,128,512]{1,2,0:T(8,128)S(1)} all-to-all(f32[8,128,512]{1,2,0:T(8,128)S(1)} %bitcast.37), channel_id=1, replica_groups=mesh['mirror'=2,'slab'=8,'cols'=2] {'slab'}, dimensions={0} | all-to-all | bytes 4194304 | tf_op jit(solution)/shard_map/all_to_all | solution.py:37
  182.0 1.5 collective-permute-start.1
  183.5 44.6 %collective-permute-done.1 = f32[128,4096]{0,1:T(8,128)S(1)} collective-permute-done((f32[128,4096]{0,1:T(8,128)S(1)}, f32[128,4096]{0,1:T(8,128)S(1)}, u32[]{:S(2)}, u32[]{:S(2)}) %collective-permute-start.1) | collective-permute-done | bytes 2097184 | tf_op jit(solution)/shard_map/ppermute | solution.py:10
  228.0 0.3 add_bitcast_fusion
  228.3 1.8 copy.15
Async XLA Ops:
  1.9 48.8 %collective-permute-start = (f32[128,4096]{0,1:T(8,128)S(1)}, f32[128,4096]{0,1:T(8,128)}, u32[]{:S(2)}, u32[]{:S(2)}) collective-permute-start(f32[128,4096]{0,1:T(8,128)S(1)} %bitcast.33), channel_id=1, source_target_pairs={{0,16},{16,0},{1,17},{17,1},{2,18},{18,2},{3,19},{19,3},{4,20},{20... | collective-permute-start | bytes 6291464 | tf_op jit(solution)/shard_map/ppermute | solution.py:10
  107.9 15.6 %copy-start = (f32[1,1024,1024]{2,1,0:T(8,128)S(1)}, f32[1,1024,1024]{2,1,0:T(8,128)}, u32[]{:S(2)}) copy-start(f32[1,1024,1024]{2,1,0:T(8,128)} %param.7) | copy-start | bytes 12582916
  107.9 15.6 %copy-start.1 = (f32[1,1024]{1,0:T(1,128)S(1)}, f32[1,1024]{1,0:T(1,128)}, u32[]{:S(2)}) copy-start(f32[1,1024]{1,0:T(1,128)} %param.8) | copy-start | bytes 12292
  108.0 15.6 %copy-start.2 = (f32[512]{0:T(512)S(1)}, f32[512]{0:T(512)}, u32[]{:S(2)}) copy-start(f32[512]{0:T(512)} %param.9) | copy-start | bytes 6148
  182.0 46.1 %collective-permute-start.1 = (f32[128,4096]{0,1:T(8,128)S(1)}, f32[128,4096]{0,1:T(8,128)S(1)}, u32[]{:S(2)}, u32[]{:S(2)}) collective-permute-start(f32[128,4096]{0,1:T(8,128)S(1)} %bitcast.34), channel_id=1, source_target_pairs={{0,16},{16,0},{1,17},{17,1},{2,18},{18,2},{3,19},{19,3},{4,20},{20... | collective-permute-start | bytes 6291464 | tf_op jit(solution)/shard_map/ppermute | solution.py:10
where the time goes:
time: 230 us
  blocking collectives  105 us (46%)
  waiting for transfers between devices  90.3 us (39%)
  matrix products  22.7 us (10%)
  local copies, waits for them, and re-layouts  5.8 us (3%)
  starting transfers between devices  4.55 us (2%)
    ppermute x2, waiting for transfers between devices, from_partner(): return lax.ppermute(value, axis, pairs)  90.3 us
    all_to_all x1, blocking collectives, shards(): lax.all_to_all(folded, 'slab', split_axis=1, concat_axis=0, tiled=True)  53.4 us
    all_to_all x1, blocking collectives, shards(): lax.all_to_all(solved, 'slab', split_axis=0, concat_axis=1, tiled=True)  51.1 us
    dot_general x1, matrix products, project(): jnp.dot(analysis, column_field, precision=lax.Precision.HIGHEST, preferre...  15.6 us
    dot_general x1, matrix products, project(): jnp.dot(synthesis, scaled, precision=lax.Precision.HIGHEST, preferred_ele...  7.08 us
  transfers between devices with their start and end apart: 2, of which 2 were waited for; matrix products, arithmetic and copies ran while one was open for 0% of the time, Pallas kernels for 0%

commit v1 on v0

v1 whole, which is shorter than its diff:
```python
import functools

import jax
import jax.numpy as jnp
from jax import lax
from jax.experimental import pallas as pl
from jax.experimental.pallas import tpu as pltpu
from jax.sharding import PartitionSpec as P

MESH = pl.DeviceIdType.MESH
PAIRS = 2
TILE = 256
SWAP_A, SPREAD_A, SPREAD_B, SWAP_B, BACK_SWAP_B, BACK_SPREAD_B, BACK_SPREAD_A, BACK_SWAP_A = range(8)
GROUPS = 8


def split(value):
    high = value.astype(jnp.bfloat16)
    return high, (value - high.astype(jnp.float32)).astype(jnp.bfloat16)


def kernel(
    n,
    field,
    analysis,
    synthesis,
    eigen,
    wave,
    out,
    own,
    staged,
    matrices,
    swapped_a,
    folded_a,
    landed_a,
    landed_b,
    swapped_b,
    right,
    scaled,
    solved_a,
    solved_b,
    back_a,
    back_swapped_a,
    back_swapped_b,
    combined_b,
    combined_a,
    send_sem,
    recv_sem,
    load_sem,
    own_b_sem,
    store_sem,
):
    rows = field.shape[1]
    width = field.shape[2] // n
    w = width // (2 * PAIRS)
    height = analysis.shape[1]
    me = lax.axis_index("slab")
    parity = lax.axis_index("mirror")
    sign = (1 - 2 * parity).astype(jnp.float32)
    partner = {"mirror": 1 - parity}

    def offset(i):
        half = (i + 1) // 2
        odd = i % 2
        return n // 2 + odd * half + (1 - odd) * (n - half)

    def target(i):
        return lax.rem(me + offset(i), n)

    def source(i):
        return lax.rem(me + 2 * n - offset(i), n)

    def columns(d, k, b):
        return pl.ds(pl.multiple_of(d * width + (2 * k + b) * w, w), w)

    def remote(src, dst, k, group, sent, received, device):
        return pltpu.make_async_remote_copy(
            src_ref=src,
            dst_ref=dst,
            send_sem=send_sem.at[k * GROUPS + group, sent],
            recv_sem=recv_sem.at[k * GROUPS + group, received],
            device_id=device,
            device_id_type=MESH,
        )

    def swap(src, dst, k, group, d):
        remote(src, dst, k, group, d, d, partner).start()

    def spread(src, dst, k, group, d):
        remote(src, dst, k, group, d, me, {"slab": d}).start()

    def arrived(dst, k, group, s):
        remote(dst, dst, k, group, s, s, partner).wait_recv()

    def each(body):
        def step(i, carry):
            body(i)
            return carry

        lax.fori_loop(0, n - 1, step, 0)

    loads = [
        pltpu.make_async_copy(field.at[0], own, load_sem.at[0]),
        pltpu.make_async_copy(analysis.at[0], staged.at[0], load_sem.at[1]),
        pltpu.make_async_copy(synthesis.at[0], staged.at[1], load_sem.at[2]),
    ]
    own_b = [
        pltpu.make_async_copy(field.at[0, :, columns(me, k, 1)], landed_b.at[k, me], own_b_sem.at[k])
        for k in range(PAIRS)
    ]
    for copy in loads + own_b:
        copy.start()

    barrier = pltpu.get_barrier_semaphore()

    def greet(i):
        pl.semaphore_signal(barrier, inc=1, device_id={"slab": target(i)}, device_id_type=MESH)

    each(greet)
    pl.semaphore_signal(barrier, inc=1, device_id=partner, device_id_type=MESH)
    pl.semaphore_wait(barrier, n)

    def forward_start(k):
        def body(i):
            d = target(i)
            swap(field.at[0, :, columns(d, k, 0)], swapped_a.at[k, d], k, SWAP_A, d)
            spread(field.at[0, :, columns(d, k, 1)], landed_b.at[k, me], k, SPREAD_B, d)

        each(body)
        swap(field.at[0, :, columns(me, k, 0)], swapped_a.at[k, me], k, SWAP_A, me)
        swap(field.at[0, :, columns(me, k, 1)], swapped_b.at[k, me], k, SWAP_B, me)

    def fold_a(k, d):
        arrived(swapped_a.at[k, d], k, SWAP_A, d)
        return (swapped_a[k, d] + sign * own[:, columns(d, k, 0)]) * 0.5

    def forward_relay(k):
        def body(i):
            d = target(i)
            folded_a[k, d] = fold_a(k, d)
            spread(folded_a.at[k, d], landed_a.at[k, me], k, SPREAD_A, d)
            s = source(i)
            arrived(landed_b.at[k, s], k, SPREAD_B, s)
            swap(landed_b.at[k, s], swapped_b.at[k, s], k, SWAP_B, s)

        each(body)
        landed_a[k, me] = fold_a(k, me)
        own_b[k].wait()

    def gather(k):
        def put(s):
            block = pl.ds(pl.multiple_of(s * rows, rows), rows)
            right[0, block, :w], right[1, block, :w] = split(landed_a[k, s])
            arrived(swapped_b.at[k, s], k, SWAP_B, s)
            folded = (swapped_b[k, s] + sign * landed_b[k, s]) * 0.5
            right[0, block, w:], right[1, block, w:] = split(folded)

        put(me)

        def body(i):
            s = source(i)
            arrived(landed_a.at[k, s], k, SPREAD_A, s)
            put(s)

        each(body)

    def product(which, operand, finish):
        def step(t, carry):
            block = pl.ds(pl.multiple_of(t * TILE, TILE), TILE)
            high, low = matrices[which, 0, block, :], matrices[which, 1, block, :]
            dot = functools.partial(jnp.dot, preferred_element_type=jnp.float32)
            finish(t, block, dot(high, operand[0]) + (dot(high, operand[1]) + dot(low, operand[0])))
            return carry

        lax.fori_loop(0, height // TILE, step, 0)

    def compute(k):
        def scale(t, block, total):
            shift = jnp.broadcast_to(eigen[0:1, block], (2 * w, TILE)).T
            value = total / (shift + wave[0:1, 2 * w * k : 2 * w * (k + 1)])
            scaled[0, block, :], scaled[1, block, :] = split(value)

        def keep(t, block, total):
            per = TILE // rows
            blocks = pl.ds(t * per, per)
            solved_a[k, blocks] = -total[:, :w].reshape(per, rows, w)
            solved_b[k, blocks] = -total[:, w:].reshape(per, rows, w)

        product(0, right, scale)
        product(1, scaled, keep)

    def back_start(k):
        def body(i):
            d = target(i)
            spread(solved_a.at[k, d], back_a.at[k, me], k, BACK_SPREAD_A, d)
            swap(solved_b.at[k, d], back_swapped_b.at[k, d], k, BACK_SWAP_B, d)

        each(body)
        swap(solved_a.at[k, me], back_swapped_a.at[k, me], k, BACK_SWAP_A, me)
        swap(solved_b.at[k, me], back_swapped_b.at[k, me], k, BACK_SWAP_B, me)

    def combine_b(k, d):
        arrived(back_swapped_b.at[k, d], k, BACK_SWAP_B, d)
        combined_b[k, d] = back_swapped_b[k, d] + sign * solved_b[k, d]

    def own_back_b(k):
        return pltpu.make_async_copy(
            combined_b.at[k, me], out.at[0, :, columns(me, k, 1)], store_sem.at[k, n]
        )

    def back_relay(k):
        def body(i):
            d = target(i)
            combine_b(k, d)
            spread(combined_b.at[k, d], out.at[0, :, columns(me, k, 1)], k, BACK_SPREAD_B, d)
            s = source(i)
            arrived(back_a.at[k, s], k, BACK_SPREAD_A, s)
            swap(back_a.at[k, s], back_swapped_a.at[k, s], k, BACK_SWAP_A, s)

        each(body)
        combine_b(k, me)
        own_back_b(k).start()

    def store_a(k, s):
        return pltpu.make_async_copy(
            combined_a.at[k, s], out.at[0, :, columns(s, k, 0)], store_sem.at[k, s]
        )

    def finish(k):
        def put(s, mine):
            arrived(back_swapped_a.at[k, s], k, BACK_SWAP_A, s)
            combined_a[k, s] = back_swapped_a[k, s] + sign * mine[k, s]
            store_a(k, s).start()

        put(me, solved_a)
        each(lambda i: put(source(i), back_a))

    def drain(k):
        def body(i):
            s = source(i)
            arrived(out.at[0, :, columns(s, k, 1)], k, BACK_SPREAD_B, s)
            d = target(i)
            for group in range(GROUPS):
                remote(landed_a.at[k, d], landed_a.at[k, d], k, group, d, d, partner).wait_send()
            store_a(k, s).wait()

        each(body)
        for group in (SWAP_A, SWAP_B, BACK_SWAP_A, BACK_SWAP_B):
            remote(landed_a.at[k, me], landed_a.at[k, me], k, group, me, me, partner).wait_send()
        store_a(k, me).wait()
        own_back_b(k).wait()

    forward_start(0)

    for copy in loads:
        copy.wait()

    def halve(t, carry):
        block = pl.ds(pl.multiple_of(t * TILE, TILE), TILE)
        for which in range(2):
            matrices[which, 0, block, :], matrices[which, 1, block, :] = split(staged[which, block, :])
        return carry

    lax.fori_loop(0, height // TILE, halve, 0)

    for k in range(PAIRS):
        forward_relay(k)
        if k + 1 < PAIRS:
            forward_start(k + 1)
        if k > 0:
            back_start(k - 1)
        gather(k)
        compute(k)
        if k > 0:
            back_relay(k - 1)
    back_start(PAIRS - 1)
    for k in range(PAIRS - 1):
        finish(k)
    back_relay(PAIRS - 1)
    finish(PAIRS - 1)
    for k in range(PAIRS):
        drain(k)


def shards(n, right_side, analysis, synthesis, negated_eigen, wave_square):
    rows, modes = right_side.shape[1:]
    height = analysis.shape[1]
    width = modes // n
    w = width // (2 * PAIRS)
    pieces = pltpu.VMEM((PAIRS, n, rows, w), jnp.float32)
    anywhere = pl.BlockSpec(memory_space=pl.ANY)
    vmem = pl.BlockSpec(memory_space=pltpu.VMEM)
    return pl.pallas_call(
        functools.partial(kernel, n),
        out_shape=jax.ShapeDtypeStruct(right_side.shape, jnp.float32),
        in_specs=[anywhere, anywhere, anywhere, vmem, vmem],
        out_specs=anywhere,
        scratch_shapes=[
            pltpu.VMEM((rows, modes), jnp.float32),
            pltpu.VMEM((2, height, height), jnp.float32),
            pltpu.VMEM((2, 2, height, height), jnp.bfloat16),
        ]
        + [pieces] * 5
        + [pltpu.VMEM((2, height, 2 * w), jnp.bfloat16)] * 2
        + [pieces] * 7
        + [
            pltpu.SemaphoreType.DMA((PAIRS * GROUPS, n)),
            pltpu.SemaphoreType.DMA((PAIRS * GROUPS, n)),
            pltpu.SemaphoreType.DMA((3,)),
            pltpu.SemaphoreType.DMA((PAIRS,)),
            pltpu.SemaphoreType.DMA((PAIRS, n + 1)),
        ],
        compiler_params=pltpu.CompilerParams(
            collective_id=0, has_side_effects=True, vmem_limit_bytes=56 * 2**20
        ),
    )(right_side, analysis, synthesis, negated_eigen, wave_square[None])


def solution(mesh):
    return jax.shard_map(
        functools.partial(shards, mesh.shape["slab"]),
        mesh=mesh,
        in_specs=(
            P("mirror", "slab", "cols"),
            P("mirror", None, None),
            P("mirror", None, None),
            P("mirror", None),
            P(("cols", "slab")),
        ),
        out_specs=P("mirror", "slab", "cols"),
        check_vma=False,
    )
```

time: 230 us -> 105 us (0.46)
  blocking collectives: 105 us -> 0 us
  Pallas kernels: 0 us -> 102 us
  waiting for transfers between devices: 90.3 us -> 0 us
  matrix products: 22.7 us -> 0 us
  starting transfers between devices: 4.55 us -> 0 us
  local copies, waits for them, and re-layouts: 5.8 us -> 3.11 us
    all_to_all x2 -> x0, blocking collectives: 105 us -> none  [the longest x1 53.4 us: shards(): lax.all_to_all(folded, 'slab', split_axis=1, concat_axis=0, tiled=True)]
    pallas_call x0 -> x1, Pallas kernels: none -> 102 us  [shards(): pl.pallas_call(functools.partial(kernel, n), out_shape=jax.ShapeDtypeStru...]
    ppermute x2 -> x0, waiting for transfers between devices: 90.3 us -> none  [from_partner(): return lax.ppermute(value, axis, pairs)]
    dot_general x2 -> x0, matrix products: 22.7 us -> none  [the longest x1 15.6 us: project(): jnp.dot(analysis, column_field, precision=lax.Precision.HIGHEST, preferre...]
    ppermute x2 -> x0, starting transfers between devices: 4.55 us -> none  [from_partner(): return lax.ppermute(value, axis, pairs)]
  transfers between devices with their start and end apart: 2 -> 0, of which waited for: 2 -> 0; matrix products, arithmetic and copies ran while one was open for 0% -> 0% of each run, Pallas kernels for 0% -> 0%
where the time goes in v1:
time: 105 us
  Pallas kernels  102 us (97%)
  local copies, waits for them, and re-layouts  3.11 us (3%)
    pallas_call x1, Pallas kernels, shards(): pl.pallas_call(functools.partial(kernel, n), out_shape=jax.ShapeDtypeStru...  102 us
    unnamed x1, local copies, waits for them, and re-layouts  3.11 us

profile of v1, /device:TPU:0, one launch (start us, length us, event | category | flops | bytes accessed | tf_op | source)
XLA Modules:
  0.0 105.0 jit_solution(16668701924997437565)
XLA Ops:
  0.0 101.8 %shard_map.55 = f32[1,128,4096]{2,1,0:T(8,128)} custom-call(f32[1,128,4096]{2,1,0:T(8,128)} %field.1, f32[1,1024,1024]{2,1,0:T(8,128)} %analysis.1, f32[1,1024,1024]{2,1,0:T(8,128)} %synthesis.1, f32[1,1024]{1,0:T(1,128)} %eigen.1, f32[1,512]{1,0:T(1,128)} %bitcast.1), custom_call_target="tpu_custom_call" | custom-call | tf_op jit(solution)/shard_map/pallas_call | solution.py:293
  101.9 3.1 %copy.7 = f32[1,128,4096]{2,1,0:T(8,128)} copy(f32[1,128,4096]{2,1,0:T(8,128)} %shard_map.55) | data formatting | bytes 4194304

commit v2 on v1

--- a/solution.py
+++ b/solution.py
@@ -92,12 +92,17 @@
     def arrived(dst, k, group, s):
         remote(dst, dst, k, group, s, s, partner).wait_recv()
 
-    def each(body):
+    def each(body, start=0, stop=n - 1):
         def step(i, carry):
             body(i)
             return carry
 
-        lax.fori_loop(0, n - 1, step, 0)
+        lax.fori_loop(start, stop, step, 0)
+
+    def whole(relay):
+        body, last = relay
+        each(body)
+        last()
 
     loads = [
         pltpu.make_async_copy(field.at[0], own, load_sem.at[0]),
@@ -143,9 +148,11 @@
             arrived(landed_b.at[k, s], k, SPREAD_B, s)
             swap(landed_b.at[k, s], swapped_b.at[k, s], k, SWAP_B, s)
 
-        each(body)
-        landed_a[k, me] = fold_a(k, me)
-        own_b[k].wait()
+        def last():
+            landed_a[k, me] = fold_a(k, me)
+            own_b[k].wait()
+
+        return body, last
 
     def gather(k):
         def put(s):
@@ -164,17 +171,23 @@
 
         each(body)
 
-    def product(which, operand, finish):
+    tiles = height // TILE
+
+    def product(which, operand, finish, beside):
         def step(t, carry):
             block = pl.ds(pl.multiple_of(t * TILE, TILE), TILE)
             high, low = matrices[which, 0, block, :], matrices[which, 1, block, :]
             dot = functools.partial(jnp.dot, preferred_element_type=jnp.float32)
             finish(t, block, dot(high, operand[0]) + (dot(high, operand[1]) + dot(low, operand[0])))
+            at = which * tiles + t
+            each(beside, at * (n - 1) // (2 * tiles), (at + 1) * (n - 1) // (2 * tiles))
             return carry
 
-        lax.fori_loop(0, height // TILE, step, 0)
-
-    def compute(k):
+        lax.fori_loop(0, tiles, step, 0)
+
+    def compute(k, relay):
+        beside, last = relay
+
         def scale(t, block, total):
             shift = jnp.broadcast_to(eigen[0:1, block], (2 * w, TILE)).T
             value = total / (shift + wave[0:1, 2 * w * k : 2 * w * (k + 1)])
@@ -186,8 +199,9 @@
             solved_a[k, blocks] = -total[:, :w].reshape(per, rows, w)
             solved_b[k, blocks] = -total[:, w:].reshape(per, rows, w)
 
-        product(0, right, scale)
-        product(1, scaled, keep)
+        product(0, right, scale, beside)
+        product(1, scaled, keep, beside)
+        last()
 
     def back_start(k):
         def body(i):
@@ -217,9 +231,11 @@
             arrived(back_a.at[k, s], k, BACK_SPREAD_A, s)
             swap(back_a.at[k, s], back_swapped_a.at[k, s], k, BACK_SWAP_A, s)
 
-        each(body)
-        combine_b(k, me)
-        own_back_b(k).start()
+        def last():
+            combine_b(k, me)
+            own_back_b(k).start()
+
+        return body, last
 
     def store_a(k, s):
         return pltpu.make_async_copy(
@@ -261,23 +277,19 @@
             matrices[which, 0, block, :], matrices[which, 1, block, :] = split(staged[which, block, :])
         return carry
 
-    lax.fori_loop(0, height // TILE, halve, 0)
-
-    for k in range(PAIRS):
-        forward_relay(k)
-        if k + 1 < PAIRS:
-            forward_start(k + 1)
-        if k > 0:
-            back_start(k - 1)
-        gather(k)
-        compute(k)
-        if k > 0:
-            back_relay(k - 1)
-    back_start(PAIRS - 1)
-    for k in range(PAIRS - 1):
-        finish(k)
-    back_relay(PAIRS - 1)
-    finish(PAIRS - 1)
+    lax.fori_loop(0, tiles, halve, 0)
+
+    whole(forward_relay(0))
+    forward_start(1)
+    gather(0)
+    compute(0, forward_relay(1))
+    back_start(0)
+    gather(1)
+    compute(1, back_relay(0))
+    back_start(1)
+    whole(back_relay(1))
+    finish(0)
+    finish(1)
     for k in range(PAIRS):
         drain(k)
 
@@ -287,6 +299,7 @@
     height = analysis.shape[1]
     width = modes // n
     w = width // (2 * PAIRS)
+    scratch_bytes = 4 * (modes * rows * 7 + height * height * 4 + height * w * 4)
     pieces = pltpu.VMEM((PAIRS, n, rows, w), jnp.float32)
     anywhere = pl.BlockSpec(memory_space=pl.ANY)
     vmem = pl.BlockSpec(memory_space=pltpu.VMEM)
@@ -311,7 +324,7 @@
             pltpu.SemaphoreType.DMA((PAIRS, n + 1)),
         ],
         compiler_params=pltpu.CompilerParams(
-            collective_id=0, has_side_effects=True, vmem_limit_bytes=56 * 2**20
+            collective_id=0, has_side_effects=True, vmem_limit_bytes=scratch_bytes + 4 * 2**20
         ),
     )(right_side, analysis, synthesis, negated_eigen, wave_square[None])
 

time: 105 us -> 111 us (1.057)
  local copies, waits for them, and re-layouts: 3.11 us -> 8.65 us
    unnamed x1 -> x11, local copies, waits for them, and re-layouts: 3.11 us -> 8.65 us
where the time goes in v2:
time: 111 us; the launch traced here: 110 us
  Pallas kernels  102 us (92%)
  local copies, waits for them, and re-layouts  8.65 us (8%)
    pallas_call x1, Pallas kernels, shards(): pl.pallas_call(functools.partial(kernel, n), out_shape=jax.ShapeDtypeStru...  102 us
    unnamed x11, local copies, waits for them, and re-layouts  8.65 us

profile of v2, /device:TPU:0, one launch (start us, length us, event | category | flops | bytes accessed | tf_op | source)
XLA Modules:
  0.0 110.4 jit_solution(11422609937698357912)
XLA Ops:
  0.0 0.0 copy-start
  0.0 2.2 %copy-done = f32[1,1024,1024]{2,1,0:T(8,128)S(1)} copy-done((f32[1,1024,1024]{2,1,0:T(8,128)S(1)}, f32[1,1024,1024]{2,1,0:T(8,128)}, u32[]{:S(2)}) %copy-start) | copy-done | bytes 4194328
  2.2 0.0 copy-start.1
  2.2 2.2 %copy-done.1 = f32[1,1024,1024]{2,1,0:T(8,128)S(1)} copy-done((f32[1,1024,1024]{2,1,0:T(8,128)S(1)}, f32[1,1024,1024]{2,1,0:T(8,128)}, u32[]{:S(2)}) %copy-start.1) | copy-done | bytes 4194328
  4.4 0.0 copy-start.2
  4.4 1.6 %copy-done.2 = f32[1,128,4096]{2,1,0:T(8,128)S(1)} copy-done((f32[1,128,4096]{2,1,0:T(8,128)S(1)}, f32[1,128,4096]{2,1,0:T(8,128)}, u32[]{:S(2)}) %copy-start.2) | copy-done | bytes 2097176
  6.0 0.0 copy-start.3
  6.0 0.7 copy-done.3
  6.7 0.0 copy-start.4
  6.7 0.7 copy-done.4
  7.3 101.7 %shard_map.55 = f32[1,128,4096]{2,1,0:T(8,128)S(1)} custom-call(f32[1,128,4096]{2,1,0:T(8,128)S(1)} %copy-done.2, f32[1,1024,1024]{2,1,0:T(8,128)S(1)} %copy-done, f32[1,1024,1024]{2,1,0:T(8,128)S(1)} %copy-done.1, f32[1,1024]{1,0:T(1,128)S(1)} %copy-done.3, f32[1,512]{1,0:T(1,128)S(1)} %bitcast.1), custom_call_target="tpu_custom_call" | custom-call | tf_op jit(solution)/shard_map/pallas_call | solution.py:306
  109.1 1.3 %copy.7 = f32[1,128,4096]{2,1,0:T(8,128)} copy(f32[1,128,4096]{2,1,0:T(8,128)S(1)} %shard_map.55) | data formatting | bytes 4194304
Async XLA Ops:
  0.0 2.2 %copy-start = (f32[1,1024,1024]{2,1,0:T(8,128)S(1)}, f32[1,1024,1024]{2,1,0:T(8,128)}, u32[]{:S(2)}) copy-start(f32[1,1024,1024]{2,1,0:T(8,128)} %analysis.1) | copy-start | bytes 12582916
  2.2 2.2 %copy-start.1 = (f32[1,1024,1024]{2,1,0:T(8,128)S(1)}, f32[1,1024,1024]{2,1,0:T(8,128)}, u32[]{:S(2)}) copy-start(f32[1,1024,1024]{2,1,0:T(8,128)} %synthesis.1) | copy-start | bytes 12582916
  4.4 1.6 %copy-start.2 = (f32[1,128,4096]{2,1,0:T(8,128)S(1)}, f32[1,128,4096]{2,1,0:T(8,128)}, u32[]{:S(2)}) copy-start(f32[1,128,4096]{2,1,0:T(8,128)} %field.1) | copy-start | bytes 6291460
  6.0 0.7 copy-start.3
  6.7 0.7 copy-start.4

commit v3 on v2

--- a/solution.py
+++ b/solution.py
@@ -24,8 +24,8 @@
     field,
     analysis,
     synthesis,
-    eigen,
-    wave,
+    eigen_in,
+    wave_in,
     out,
     own,
     staged,
@@ -44,6 +44,8 @@
     back_swapped_b,
     combined_b,
     combined_a,
+    eigen,
+    wave,
     send_sem,
     recv_sem,
     load_sem,
@@ -60,9 +62,11 @@
     partner = {"mirror": 1 - parity}
 
     def offset(i):
-        half = (i + 1) // 2
-        odd = i % 2
-        return n // 2 + odd * half + (1 - odd) * (n - half)
+        j = i // 2
+        step = (j + 1) // 2
+        far = n // 2 + (j % 2) * step + (1 - j % 2) * (n - step)
+        near = (1 - j % 2) * (j // 2 + 1) + (j % 2) * (n - step)
+        return lax.rem((1 - i % 2) * far + (i % 2) * near, n)
 
     def target(i):
         return lax.rem(me + offset(i), n)
@@ -108,6 +112,8 @@
         pltpu.make_async_copy(field.at[0], own, load_sem.at[0]),
         pltpu.make_async_copy(analysis.at[0], staged.at[0], load_sem.at[1]),
         pltpu.make_async_copy(synthesis.at[0], staged.at[1], load_sem.at[2]),
+        pltpu.make_async_copy(eigen_in, eigen, load_sem.at[3]),
+        pltpu.make_async_copy(wave_in, wave, load_sem.at[4]),
     ]
     own_b = [
         pltpu.make_async_copy(field.at[0, :, columns(me, k, 1)], landed_b.at[k, me], own_b_sem.at[k])
@@ -302,11 +308,11 @@
     scratch_bytes = 4 * (modes * rows * 7 + height * height * 4 + height * w * 4)
     pieces = pltpu.VMEM((PAIRS, n, rows, w), jnp.float32)
     anywhere = pl.BlockSpec(memory_space=pl.ANY)
-    vmem = pl.BlockSpec(memory_space=pltpu.VMEM)
+    hbm = pl.BlockSpec(memory_space=pltpu.HBM)
     return pl.pallas_call(
         functools.partial(kernel, n),
         out_shape=jax.ShapeDtypeStruct(right_side.shape, jnp.float32),
-        in_specs=[anywhere, anywhere, anywhere, vmem, vmem],
+        in_specs=[hbm] * 5,
         out_specs=anywhere,
         scratch_shapes=[
             pltpu.VMEM((rows, modes), jnp.float32),
@@ -317,9 +323,11 @@
         + [pltpu.VMEM((2, height, 2 * w), jnp.bfloat16)] * 2
         + [pieces] * 7
         + [
+            pltpu.VMEM((1, height), jnp.float32),
+            pltpu.VMEM((1, width), jnp.float32),
             pltpu.SemaphoreType.DMA((PAIRS * GROUPS, n)),
             pltpu.SemaphoreType.DMA((PAIRS * GROUPS, n)),
-            pltpu.SemaphoreType.DMA((3,)),
+            pltpu.SemaphoreType.DMA((5,)),
             pltpu.SemaphoreType.DMA((PAIRS,)),
             pltpu.SemaphoreType.DMA((PAIRS, n + 1)),
         ],

time: 111 us -> 111 us (level)
  no operation moved by 1% of the time
where the time goes in v3:
time: 111 us; the launch traced here: 110 us
  Pallas kernels  102 us (92%)
  local copies, waits for them, and re-layouts  8.65 us (8%)
    pallas_call x1, Pallas kernels, shards(): pl.pallas_call(functools.partial(kernel, n), out_shape=jax.ShapeDtypeStru...  102 us
    unnamed x11, local copies, waits for them, and re-layouts  8.65 us

profile of v3, /device:TPU:0, one launch (start us, length us, event | category | flops | bytes accessed | tf_op | source)
XLA Modules:
  0.0 110.5 jit_solution(7426020168795011319)
XLA Ops:
  0.0 0.0 copy-start
  0.0 2.2 %copy-done = f32[1,1024,1024]{2,1,0:T(8,128)S(1)} copy-done((f32[1,1024,1024]{2,1,0:T(8,128)S(1)}, f32[1,1024,1024]{2,1,0:T(8,128)}, u32[]{:S(2)}) %copy-start) | copy-done | bytes 4194328
  2.2 0.0 copy-start.1
  2.2 2.2 %copy-done.1 = f32[1,1024,1024]{2,1,0:T(8,128)S(1)} copy-done((f32[1,1024,1024]{2,1,0:T(8,128)S(1)}, f32[1,1024,1024]{2,1,0:T(8,128)}, u32[]{:S(2)}) %copy-start.1) | copy-done | bytes 4194328
  4.4 0.0 copy-start.2
  4.4 1.6 %copy-done.2 = f32[1,128,4096]{2,1,0:T(8,128)S(1)} copy-done((f32[1,128,4096]{2,1,0:T(8,128)S(1)}, f32[1,128,4096]{2,1,0:T(8,128)}, u32[]{:S(2)}) %copy-start.2) | copy-done | bytes 2097176
  6.0 0.0 copy-start.3
  6.0 0.7 copy-done.3
  6.7 0.0 copy-start.4
  6.7 0.7 copy-done.4
  7.3 101.8 %shard_map.55 = f32[1,128,4096]{2,1,0:T(8,128)S(1)} custom-call(f32[1,128,4096]{2,1,0:T(8,128)S(1)} %copy-done.2, f32[1,1024,1024]{2,1,0:T(8,128)S(1)} %copy-done, f32[1,1024,1024]{2,1,0:T(8,128)S(1)} %copy-done.1, f32[1,1024]{1,0:T(1,128)S(1)} %copy-done.3, f32[1,512]{1,0:T(1,128)S(1)} %bitcast.1), custom_call_target="tpu_custom_call" | custom-call | tf_op jit(solution)/shard_map/pallas_call | solution.py:312
  109.2 1.3 %copy.7 = f32[1,128,4096]{2,1,0:T(8,128)} copy(f32[1,128,4096]{2,1,0:T(8,128)S(1)} %shard_map.55) | data formatting | bytes 4194304
Async XLA Ops:
  0.0 2.2 %copy-start = (f32[1,1024,1024]{2,1,0:T(8,128)S(1)}, f32[1,1024,1024]{2,1,0:T(8,128)}, u32[]{:S(2)}) copy-start(f32[1,1024,1024]{2,1,0:T(8,128)} %analysis.1) | copy-start | bytes 12582916
  2.2 2.2 %copy-start.1 = (f32[1,1024,1024]{2,1,0:T(8,128)S(1)}, f32[1,1024,1024]{2,1,0:T(8,128)}, u32[]{:S(2)}) copy-start(f32[1,1024,1024]{2,1,0:T(8,128)} %synthesis.1) | copy-start | bytes 12582916
  4.4 1.6 %copy-start.2 = (f32[1,128,4096]{2,1,0:T(8,128)S(1)}, f32[1,128,4096]{2,1,0:T(8,128)}, u32[]{:S(2)}) copy-start(f32[1,128,4096]{2,1,0:T(8,128)} %field.1) | copy-start | bytes 6291460
  6.0 0.7 copy-start.3
  6.7 0.7 copy-start.4

commit v4 on v3

--- a/solution.py
+++ b/solution.py
@@ -62,11 +62,9 @@
     partner = {"mirror": 1 - parity}
 
     def offset(i):
-        j = i // 2
-        step = (j + 1) // 2
-        far = n // 2 + (j % 2) * step + (1 - j % 2) * (n - step)
-        near = (1 - j % 2) * (j // 2 + 1) + (j % 2) * (n - step)
-        return lax.rem((1 - i % 2) * far + (i % 2) * near, n)
+        half = (i + 1) // 2
+        odd = i % 2
+        return n // 2 + odd * half + (1 - odd) * (n - half)
 
     def target(i):
         return lax.rem(me + offset(i), n)
@@ -119,9 +117,6 @@
         pltpu.make_async_copy(field.at[0, :, columns(me, k, 1)], landed_b.at[k, me], own_b_sem.at[k])
         for k in range(PAIRS)
     ]
-    for copy in loads + own_b:
-        copy.start()
-
     barrier = pltpu.get_barrier_semaphore()
 
     def greet(i):
@@ -273,9 +268,8 @@
         own_back_b(k).wait()
 
     forward_start(0)
-
-    for copy in loads:
-        copy.wait()
+    for copy in loads + own_b:
+        copy.start()
 
     def halve(t, carry):
         block = pl.ds(pl.multiple_of(t * TILE, TILE), TILE)
@@ -283,10 +277,12 @@
             matrices[which, 0, block, :], matrices[which, 1, block, :] = split(staged[which, block, :])
         return carry
 
-    lax.fori_loop(0, tiles, halve, 0)
-
+    loads[0].wait()
     whole(forward_relay(0))
     forward_start(1)
+    for copy in loads[1:]:
+        copy.wait()
+    lax.fori_loop(0, tiles, halve, 0)
     gather(0)
     compute(0, forward_relay(1))
     back_start(0)
@@ -334,7 +330,10 @@
         compiler_params=pltpu.CompilerParams(
             collective_id=0, has_side_effects=True, vmem_limit_bytes=scratch_bytes + 4 * 2**20
         ),
-    )(right_side, analysis, synthesis, negated_eigen, wave_square[None])
+    )(*(
+        pltpu.with_memory_space_constraint(value, pltpu.HBM)
+        for value in (right_side, analysis, synthesis, negated_eigen, wave_square[None])
+    ))
 
 
 def solution(mesh):

time: 111 us -> 103 us (0.928)
  local copies, waits for them, and re-layouts: 8.65 us -> 1.32 us
    unnamed x11 -> x1, local copies, waits for them, and re-layouts: 8.65 us -> 1.32 us
where the time goes in v4:
time: 103 us; the launch traced here: 102 us
  Pallas kernels  101 us (98%)
  local copies, waits for them, and re-layouts  1.32 us (1%)
    pallas_call x1, Pallas kernels, shards(): pl.pallas_call(functools.partial(kernel, n), out_shape=jax.ShapeDtypeStru...  101 us

profile of v4, /device:TPU:0, one launch (start us, length us, event | category | flops | bytes accessed | tf_op | source)
XLA Modules:
  0.0 102.4 jit_solution(845567225412069059)
XLA Ops:
  0.0 101.0 %shard_map.55 = f32[1,128,4096]{2,1,0:T(8,128)S(1)} custom-call(f32[1,128,4096]{2,1,0:T(8,128)} %field.1, f32[1,1024,1024]{2,1,0:T(8,128)} %analysis.1, f32[1,1024,1024]{2,1,0:T(8,128)} %synthesis.1, f32[1,1024]{1,0:T(1,128)} %eigen_in.1, f32[1,512]{1,0:T(1,128)} %bitcast.1), custom_call_target="tpu_custom_call" | custom-call | tf_op jit(solution)/shard_map/pallas_call | solution.py:308
  101.1 1.3 %copy.7 = f32[1,128,4096]{2,1,0:T(8,128)} copy(f32[1,128,4096]{2,1,0:T(8,128)S(1)} %shard_map.55) | data formatting | bytes 4194304

commit v5 on v4

--- a/solution.py
+++ b/solution.py
@@ -145,7 +145,7 @@
             d = target(i)
             folded_a[k, d] = fold_a(k, d)
             spread(folded_a.at[k, d], landed_a.at[k, me], k, SPREAD_A, d)
-            s = source(i)
+            s = source(n - 2 - i)
             arrived(landed_b.at[k, s], k, SPREAD_B, s)
             swap(landed_b.at[k, s], swapped_b.at[k, s], k, SWAP_B, s)
 
@@ -228,7 +228,7 @@
             d = target(i)
             combine_b(k, d)
             spread(combined_b.at[k, d], out.at[0, :, columns(me, k, 1)], k, BACK_SPREAD_B, d)
-            s = source(i)
+            s = source(n - 2 - i)
             arrived(back_a.at[k, s], k, BACK_SPREAD_A, s)
             swap(back_a.at[k, s], back_swapped_a.at[k, s], k, BACK_SWAP_A, s)
 
@@ -278,8 +278,11 @@
         return carry
 
     loads[0].wait()
-    whole(forward_relay(0))
+    relay, last = forward_relay(0)
+    each(relay, 0, n // 2)
     forward_start(1)
+    each(relay, n // 2)
+    last()
     for copy in loads[1:]:
         copy.wait()
     lax.fori_loop(0, tiles, halve, 0)

time: 103 us -> 111 us (1.078)
  the two profiles are of different devices: /device:TPU:0 before, /device:TPU:16 now
where the time goes in v5:
time: 111 us
  Pallas kernels  109 us (98%)
  local copies, waits for them, and re-layouts  1.32 us (1%)
    pallas_call x1, Pallas kernels, shards(): pl.pallas_call(functools.partial(kernel, n), out_shape=jax.ShapeDtypeStru...  109 us

profile of v5, /device:TPU:16, one launch (start us, length us, event | category | flops | bytes accessed | tf_op | source)
XLA Modules:
  0.0 110.6 jit_solution(11677658589249170186)
XLA Ops:
  0.0 109.2 %shard_map.55 = f32[1,128,4096]{2,1,0:T(8,128)S(1)} custom-call(f32[1,128,4096]{2,1,0:T(8,128)} %field.1, f32[1,1024,1024]{2,1,0:T(8,128)} %analysis.1, f32[1,1024,1024]{2,1,0:T(8,128)} %synthesis.1, f32[1,1024]{1,0:T(1,128)} %eigen_in.1, f32[1,512]{1,0:T(1,128)} %bitcast.1), custom_call_target="tpu_custom_call" | custom-call | tf_op jit(solution)/shard_map/pallas_call | solution.py:311
  109.3 1.3 %copy.7 = f32[1,128,4096]{2,1,0:T(8,128)} copy(f32[1,128,4096]{2,1,0:T(8,128)S(1)} %shard_map.55) | data formatting | bytes 4194304

commit v6 on v4

--- a/solution.py
+++ b/solution.py
@@ -75,24 +75,24 @@
     def columns(d, k, b):
         return pl.ds(pl.multiple_of(d * width + (2 * k + b) * w, w), w)
 
-    def remote(src, dst, k, group, sent, received, device):
+    def remote(src, dst, k, group, received, device):
         return pltpu.make_async_remote_copy(
             src_ref=src,
             dst_ref=dst,
-            send_sem=send_sem.at[k * GROUPS + group, sent],
+            send_sem=send_sem.at[k * GROUPS + group],
             recv_sem=recv_sem.at[k * GROUPS + group, received],
             device_id=device,
             device_id_type=MESH,
         )
 
     def swap(src, dst, k, group, d):
-        remote(src, dst, k, group, d, d, partner).start()
+        remote(src, dst, k, group, d, partner).start()
 
     def spread(src, dst, k, group, d):
-        remote(src, dst, k, group, d, me, {"slab": d}).start()
+        remote(src, dst, k, group, me, {"slab": d}).start()
 
     def arrived(dst, k, group, s):
-        remote(dst, dst, k, group, s, s, partner).wait_recv()
+        remote(dst, dst, k, group, s, partner).wait_recv()
 
     def each(body, start=0, stop=n - 1):
         def step(i, carry):
@@ -252,18 +252,19 @@
         put(me, solved_a)
         each(lambda i: put(source(i), back_a))
 
+    def sent(k, *groups):
+        for group in groups:
+            swaps = group in (SWAP_A, SWAP_B, BACK_SWAP_A, BACK_SWAP_B)
+            pieces = landed_a.at[k, pl.ds(0, n if swaps else n - 1)]
+            remote(pieces, pieces, k, group, 0, partner).wait_send()
+
     def drain(k):
         def body(i):
             s = source(i)
             arrived(out.at[0, :, columns(s, k, 1)], k, BACK_SPREAD_B, s)
-            d = target(i)
-            for group in range(GROUPS):
-                remote(landed_a.at[k, d], landed_a.at[k, d], k, group, d, d, partner).wait_send()
             store_a(k, s).wait()
 
         each(body)
-        for group in (SWAP_A, SWAP_B, BACK_SWAP_A, BACK_SWAP_B):
-            remote(landed_a.at[k, me], landed_a.at[k, me], k, group, me, me, partner).wait_send()
         store_a(k, me).wait()
         own_back_b(k).wait()
 
@@ -289,11 +290,16 @@
     gather(1)
     compute(1, back_relay(0))
     back_start(1)
+    for k in range(PAIRS):
+        sent(k, SWAP_A, SPREAD_A, SPREAD_B, SWAP_B)
     whole(back_relay(1))
     finish(0)
+    sent(0, BACK_SWAP_B, BACK_SPREAD_B, BACK_SPREAD_A, BACK_SWAP_A)
+    drain(0)
+    sent(1, BACK_SWAP_B, BACK_SPREAD_A)
     finish(1)
-    for k in range(PAIRS):
-        drain(k)
+    drain(1)
+    sent(1, BACK_SPREAD_B, BACK_SWAP_A)
 
 
 def shards(n, right_side, analysis, synthesis, negated_eigen, wave_square):
@@ -321,7 +327,7 @@
         + [
             pltpu.VMEM((1, height), jnp.float32),
             pltpu.VMEM((1, width), jnp.float32),
-            pltpu.SemaphoreType.DMA((PAIRS * GROUPS, n)),
+            pltpu.SemaphoreType.DMA((PAIRS * GROUPS,)),
             pltpu.SemaphoreType.DMA((PAIRS * GROUPS, n)),
             pltpu.SemaphoreType.DMA((5,)),
             pltpu.SemaphoreType.DMA((PAIRS,)),

time: 103 us -> 101 us (0.981)
  Pallas kernels: 101 us -> 99.7 us
    pallas_call x1, Pallas kernels: 101 us -> 99.7 us  [shards(): pl.pallas_call(functools.partial(kernel, n), out_shape=jax.ShapeDtypeStru...]
where the time goes in v6:
time: 101 us
  Pallas kernels  99.7 us (99%)
  local copies, waits for them, and re-layouts  1.32 us (1%)
    pallas_call x1, Pallas kernels, shards(): pl.pallas_call(functools.partial(kernel, n), out_shape=jax.ShapeDtypeStru...  99.7 us

profile of v6, /device:TPU:0, one launch (start us, length us, event | category | flops | bytes accessed | tf_op | source)
XLA Modules:
  0.0 101.0 jit_solution(9435849460163667373)
XLA Ops:
  0.0 99.7 %shard_map.55 = f32[1,128,4096]{2,1,0:T(8,128)S(1)} custom-call(f32[1,128,4096]{2,1,0:T(8,128)} %field.1, f32[1,1024,1024]{2,1,0:T(8,128)} %analysis.1, f32[1,1024,1024]{2,1,0:T(8,128)} %synthesis.1, f32[1,1024]{1,0:T(1,128)} %eigen_in.1, f32[1,512]{1,0:T(1,128)} %bitcast.1), custom_call_target="tpu_custom_call" | custom-call | tf_op jit(solution)/shard_map/pallas_call | solution.py:314
  99.7 1.3 %copy.7 = f32[1,128,4096]{2,1,0:T(8,128)} copy(f32[1,128,4096]{2,1,0:T(8,128)S(1)} %shard_map.55) | data formatting | bytes 4194304

commit v7 on v6

--- a/solution.py
+++ b/solution.py
@@ -61,16 +61,13 @@
     sign = (1 - 2 * parity).astype(jnp.float32)
     partner = {"mirror": 1 - parity}
 
-    def offset(i):
-        half = (i + 1) // 2
-        odd = i % 2
-        return n // 2 + odd * half + (1 - odd) * (n - half)
+    digits = [2**b for b in range(n.bit_length() - 1)]
+    flips = [digit * (1 - 2 * lax.rem(lax.div(me, digit), 2)) for digit in digits]
 
     def target(i):
-        return lax.rem(me + offset(i), n)
-
-    def source(i):
-        return lax.rem(me + 2 * n - offset(i), n)
+        j, odd = lax.div(i, 2), lax.rem(i, 2)
+        mask = (1 - odd) * (n // 2 + j) + odd * (j + 1)
+        return me + sum(lax.rem(lax.div(mask, digit), 2) * flip for digit, flip in zip(digits, flips))
 
     def columns(d, k, b):
         return pl.ds(pl.multiple_of(d * width + (2 * k + b) * w, w), w)
@@ -145,7 +142,7 @@
             d = target(i)
             folded_a[k, d] = fold_a(k, d)
             spread(folded_a.at[k, d], landed_a.at[k, me], k, SPREAD_A, d)
-            s = source(i)
+            s = d
             arrived(landed_b.at[k, s], k, SPREAD_B, s)
             swap(landed_b.at[k, s], swapped_b.at[k, s], k, SWAP_B, s)
 
@@ -166,7 +163,7 @@
         put(me)
 
         def body(i):
-            s = source(i)
+            s = target(i)
             arrived(landed_a.at[k, s], k, SPREAD_A, s)
             put(s)
 
@@ -228,7 +225,7 @@
             d = target(i)
             combine_b(k, d)
             spread(combined_b.at[k, d], out.at[0, :, columns(me, k, 1)], k, BACK_SPREAD_B, d)
-            s = source(i)
+            s = d
             arrived(back_a.at[k, s], k, BACK_SPREAD_A, s)
             swap(back_a.at[k, s], back_swapped_a.at[k, s], k, BACK_SWAP_A, s)
 
@@ -250,7 +247,7 @@
             store_a(k, s).start()
 
         put(me, solved_a)
-        each(lambda i: put(source(i), back_a))
+        each(lambda i: put(target(i), back_a))
 
     def sent(k, *groups):
         for group in groups:
@@ -260,7 +257,7 @@
 
     def drain(k):
         def body(i):
-            s = source(i)
+            s = target(i)
             arrived(out.at[0, :, columns(s, k, 1)], k, BACK_SPREAD_B, s)
             store_a(k, s).wait()
 

time: 101 us -> 101 us (level)
  no operation moved by 1% of the time
where the time goes in v7:
time: 101 us
  Pallas kernels  99.7 us (99%)
  local copies, waits for them, and re-layouts  1.32 us (1%)
    pallas_call x1, Pallas kernels, shards(): pl.pallas_call(functools.partial(kernel, n), out_shape=jax.ShapeDtypeStru...  99.7 us

profile of v7, /device:TPU:0, one launch (start us, length us, event | category | flops | bytes accessed | tf_op | source)
XLA Modules:
  0.0 101.0 jit_solution(9475762253595963339)
XLA Ops:
  0.0 99.7 %shard_map.55 = f32[1,128,4096]{2,1,0:T(8,128)S(1)} custom-call(f32[1,128,4096]{2,1,0:T(8,128)} %field.1, f32[1,1024,1024]{2,1,0:T(8,128)} %analysis.1, f32[1,1024,1024]{2,1,0:T(8,128)} %synthesis.1, f32[1,1024]{1,0:T(1,128)} %eigen_in.1, f32[1,512]{1,0:T(1,128)} %bitcast.1), custom_call_target="tpu_custom_call" | custom-call | tf_op jit(solution)/shard_map/pallas_call | solution.py:311
  99.7 1.3 %copy.7 = f32[1,128,4096]{2,1,0:T(8,128)} copy(f32[1,128,4096]{2,1,0:T(8,128)S(1)} %shard_map.55) | data formatting | bytes 4194304

commit v8 on v6

--- a/solution.py
+++ b/solution.py
@@ -10,6 +10,7 @@
 MESH = pl.DeviceIdType.MESH
 PAIRS = 2
 TILE = 256
+STRIPS = 4
 SWAP_A, SPREAD_A, SPREAD_B, SWAP_B, BACK_SWAP_B, BACK_SPREAD_B, BACK_SPREAD_A, BACK_SWAP_A = range(8)
 GROUPS = 8
 
@@ -122,8 +123,8 @@
     def greet(i):
         pl.semaphore_signal(barrier, inc=1, device_id={"slab": target(i)}, device_id_type=MESH)
 
+    pl.semaphore_signal(barrier, inc=1, device_id=partner, device_id_type=MESH)
     each(greet)
-    pl.semaphore_signal(barrier, inc=1, device_id=partner, device_id_type=MESH)
     pl.semaphore_wait(barrier, n)
 
     def forward_start(k):
@@ -220,14 +221,16 @@
 
     def own_back_b(k):
         return pltpu.make_async_copy(
-            combined_b.at[k, me], out.at[0, :, columns(me, k, 1)], store_sem.at[k, n]
+            combined_b.at[k, me], out.at[0, :, columns(me, k, 1)], store_sem.at[k, 1]
         )
 
     def back_relay(k):
         def body(i):
             d = target(i)
             combine_b(k, d)
-            spread(combined_b.at[k, d], out.at[0, :, columns(me, k, 1)], k, BACK_SPREAD_B, d)
+            remote(
+                combined_b.at[k, d], out.at[0, :, columns(me, k, 1)], k, BACK_SPREAD_B, 0, {"slab": d}
+            ).start()
             s = source(i)
             arrived(back_a.at[k, s], k, BACK_SPREAD_A, s)
             swap(back_a.at[k, s], back_swapped_a.at[k, s], k, BACK_SWAP_A, s)
@@ -240,7 +243,7 @@
 
     def store_a(k, s):
         return pltpu.make_async_copy(
-            combined_a.at[k, s], out.at[0, :, columns(s, k, 0)], store_sem.at[k, s]
+            combined_a.at[k, s], out.at[0, :, columns(s, k, 0)], store_sem.at[k, 0]
         )
 
     def finish(k):
@@ -259,14 +262,10 @@
             remote(pieces, pieces, k, group, 0, partner).wait_send()
 
     def drain(k):
-        def body(i):
-            s = source(i)
-            arrived(out.at[0, :, columns(s, k, 1)], k, BACK_SPREAD_B, s)
-            store_a(k, s).wait()
-
-        each(body)
-        store_a(k, me).wait()
+        pieces = landed_a.at[k, pl.ds(0, n - 1)]
+        remote(pieces, pieces, k, BACK_SPREAD_B, 0, partner).wait_recv()
         own_back_b(k).wait()
+        pltpu.make_async_copy(combined_a.at[k], combined_a.at[k], store_sem.at[k, 0]).wait()
 
     forward_start(0)
     for copy in loads + own_b:
@@ -302,6 +301,20 @@
     sent(1, BACK_SPREAD_B, BACK_SWAP_A)
 
 
+def export(held, out, sem):
+    rows = held.shape[1] // STRIPS
+    copies = [
+        pltpu.make_async_copy(
+            held.at[0, pl.ds(i * rows, rows)], out.at[0, pl.ds(i * rows, rows)], sem.at[i]
+        )
+        for i in range(STRIPS)
+    ]
+    for copy in copies:
+        copy.start()
+    for copy in copies:
+        copy.wait()
+
+
 def shards(n, right_side, analysis, synthesis, negated_eigen, wave_square):
     rows, modes = right_side.shape[1:]
     height = analysis.shape[1]
@@ -311,7 +324,7 @@
     pieces = pltpu.VMEM((PAIRS, n, rows, w), jnp.float32)
     anywhere = pl.BlockSpec(memory_space=pl.ANY)
     hbm = pl.BlockSpec(memory_space=pltpu.HBM)
-    return pl.pallas_call(
+    result = pl.pallas_call(
         functools.partial(kernel, n),
         out_shape=jax.ShapeDtypeStruct(right_side.shape, jnp.float32),
         in_specs=[hbm] * 5,
@@ -331,7 +344,7 @@
             pltpu.SemaphoreType.DMA((PAIRS * GROUPS, n)),
             pltpu.SemaphoreType.DMA((5,)),
             pltpu.SemaphoreType.DMA((PAIRS,)),
-            pltpu.SemaphoreType.DMA((PAIRS, n + 1)),
+            pltpu.SemaphoreType.DMA((PAIRS, 2)),
         ],
         compiler_params=pltpu.CompilerParams(
             collective_id=0, has_side_effects=True, vmem_limit_bytes=scratch_bytes + 4 * 2**20
@@ -340,6 +353,13 @@
         pltpu.with_memory_space_constraint(value, pltpu.HBM)
         for value in (right_side, analysis, synthesis, negated_eigen, wave_square[None])
     ))
+    return pl.pallas_call(
+        export,
+        out_shape=jax.ShapeDtypeStruct(right_side.shape, jnp.float32),
+        in_specs=[anywhere],
+        out_specs=anywhere,
+        scratch_shapes=[pltpu.SemaphoreType.DMA((STRIPS,))],
+    )(result)
 
 
 def solution(mesh):

time: 101 us -> 166 us (1.64)
  Pallas kernels: 99.7 us -> 164 us
    pallas_call x0 -> x1, Pallas kernels: none -> 64.7 us  [shards(): pl.pallas_call(export, out_shape=jax.ShapeDtypeStruct(right_side.shape, j...]
where the time goes in v8:
time: 166 us; the launch traced here: 165 us
  Pallas kernels  164 us (99%)
    pallas_call x1, Pallas kernels, shards(): pl.pallas_call(functools.partial(kernel, n), out_shape=jax.ShapeDtypeStru...  99.4 us
    pallas_call x1, Pallas kernels, shards(): pl.pallas_call(export, out_shape=jax.ShapeDtypeStruct(right_side.shape, j...  64.7 us

profile of v8, /device:TPU:0, one launch (start us, length us, event | category | flops | bytes accessed | tf_op | source)
XLA Modules:
  0.0 165.4 jit_solution(15676745160682089953)
XLA Ops:
  0.0 99.4 %shard_map.55.held = f32[1,128,4096]{2,1,0:T(8,128)S(1)} custom-call(f32[1,128,4096]{2,1,0:T(8,128)} %field.1, f32[1,1024,1024]{2,1,0:T(8,128)} %analysis.1, f32[1,1024,1024]{2,1,0:T(8,128)} %synthesis.1, f32[1,1024]{1,0:T(1,128)} %eigen_in.1, f32[1,512]{1,0:T(1,128)} %bitcast.1), custom_call_target="tpu_custom_call" | custom-call | tf_op jit(solution)/shard_map/pallas_call | solution.py:327
  99.4 0.0 copy-start
  99.4 1.3 copy-done
  100.8 64.7 %shard_map.56 = f32[1,128,4096]{2,1,0:T(8,128)} custom-call(f32[1,128,4096]{2,1,0:T(8,128)} %copy-done), custom_call_target="tpu_custom_call" | custom-call | tf_op jit(solution)/shard_map/pallas_call | solution.py:356
Async XLA Ops:
  99.4 1.3 copy-start

commit v9 on v6

--- a/solution.py
+++ b/solution.py
@@ -122,8 +122,8 @@
     def greet(i):
         pl.semaphore_signal(barrier, inc=1, device_id={"slab": target(i)}, device_id_type=MESH)
 
+    pl.semaphore_signal(barrier, inc=1, device_id=partner, device_id_type=MESH)
     each(greet)
-    pl.semaphore_signal(barrier, inc=1, device_id=partner, device_id_type=MESH)
     pl.semaphore_wait(barrier, n)
 
     def forward_start(k):
@@ -220,14 +220,16 @@
 
     def own_back_b(k):
         return pltpu.make_async_copy(
-            combined_b.at[k, me], out.at[0, :, columns(me, k, 1)], store_sem.at[k, n]
+            combined_b.at[k, me], out.at[0, :, columns(me, k, 1)], store_sem.at[k, 1]
         )
 
     def back_relay(k):
         def body(i):
             d = target(i)
             combine_b(k, d)
-            spread(combined_b.at[k, d], out.at[0, :, columns(me, k, 1)], k, BACK_SPREAD_B, d)
+            remote(
+                combined_b.at[k, d], out.at[0, :, columns(me, k, 1)], k, BACK_SPREAD_B, 0, {"slab": d}
+            ).start()
             s = source(i)
             arrived(back_a.at[k, s], k, BACK_SPREAD_A, s)
             swap(back_a.at[k, s], back_swapped_a.at[k, s], k, BACK_SWAP_A, s)
@@ -240,7 +242,7 @@
 
     def store_a(k, s):
         return pltpu.make_async_copy(
-            combined_a.at[k, s], out.at[0, :, columns(s, k, 0)], store_sem.at[k, s]
+            combined_a.at[k, s], out.at[0, :, columns(s, k, 0)], store_sem.at[k, 0]
         )
 
     def finish(k):
@@ -259,14 +261,10 @@
             remote(pieces, pieces, k, group, 0, partner).wait_send()
 
     def drain(k):
-        def body(i):
-            s = source(i)
-            arrived(out.at[0, :, columns(s, k, 1)], k, BACK_SPREAD_B, s)
-            store_a(k, s).wait()
-
-        each(body)
-        store_a(k, me).wait()
+        pieces = landed_a.at[k, pl.ds(0, n - 1)]
+        remote(pieces, pieces, k, BACK_SPREAD_B, 0, partner).wait_recv()
         own_back_b(k).wait()
+        pltpu.make_async_copy(combined_a.at[k], combined_a.at[k], store_sem.at[k, 0]).wait()
 
     forward_start(0)
     for copy in loads + own_b:
@@ -331,7 +329,7 @@
             pltpu.SemaphoreType.DMA((PAIRS * GROUPS, n)),
             pltpu.SemaphoreType.DMA((5,)),
             pltpu.SemaphoreType.DMA((PAIRS,)),
-            pltpu.SemaphoreType.DMA((PAIRS, n + 1)),
+            pltpu.SemaphoreType.DMA((PAIRS, 2)),
         ],
         compiler_params=pltpu.CompilerParams(
             collective_id=0, has_side_effects=True, vmem_limit_bytes=scratch_bytes + 4 * 2**20

time: 101 us -> 101 us (level)
  no operation moved by 1% of the time
where the time goes in v9:
time: 101 us
  Pallas kernels  99.4 us (98%)
  local copies, waits for them, and re-layouts  1.32 us (1%)
    pallas_call x1, Pallas kernels, shards(): pl.pallas_call(functools.partial(kernel, n), out_shape=jax.ShapeDtypeStru...  99.4 us

profile of v9, /device:TPU:0, one launch (start us, length us, event | category | flops | bytes accessed | tf_op | source)
XLA Modules:
  0.0 100.7 jit_solution(8051324459977333576)
XLA Ops:
  0.0 99.4 %shard_map.55 = f32[1,128,4096]{2,1,0:T(8,128)S(1)} custom-call(f32[1,128,4096]{2,1,0:T(8,128)} %field.1, f32[1,1024,1024]{2,1,0:T(8,128)} %analysis.1, f32[1,1024,1024]{2,1,0:T(8,128)} %synthesis.1, f32[1,1024]{1,0:T(1,128)} %eigen_in.1, f32[1,512]{1,0:T(1,128)} %bitcast.1), custom_call_target="tpu_custom_call" | custom-call | tf_op jit(solution)/shard_map/pallas_call | solution.py:312
  99.4 1.3 %copy.7 = f32[1,128,4096]{2,1,0:T(8,128)} copy(f32[1,128,4096]{2,1,0:T(8,128)S(1)} %shard_map.55) | data formatting | bytes 4194304

commit v10 on v9

--- a/solution.py
+++ b/solution.py
@@ -142,12 +142,12 @@
 
     def forward_relay(k):
         def body(i):
+            s = source(i)
+            arrived(landed_b.at[k, s], k, SPREAD_B, s)
+            swap(landed_b.at[k, s], swapped_b.at[k, s], k, SWAP_B, s)
             d = target(i)
             folded_a[k, d] = fold_a(k, d)
             spread(folded_a.at[k, d], landed_a.at[k, me], k, SPREAD_A, d)
-            s = source(i)
-            arrived(landed_b.at[k, s], k, SPREAD_B, s)
-            swap(landed_b.at[k, s], swapped_b.at[k, s], k, SWAP_B, s)
 
         def last():
             landed_a[k, me] = fold_a(k, me)
@@ -225,14 +225,14 @@
 
     def back_relay(k):
         def body(i):
+            s = source(i)
+            arrived(back_a.at[k, s], k, BACK_SPREAD_A, s)
+            swap(back_a.at[k, s], back_swapped_a.at[k, s], k, BACK_SWAP_A, s)
             d = target(i)
             combine_b(k, d)
             remote(
                 combined_b.at[k, d], out.at[0, :, columns(me, k, 1)], k, BACK_SPREAD_B, 0, {"slab": d}
             ).start()
-            s = source(i)
-            arrived(back_a.at[k, s], k, BACK_SPREAD_A, s)
-            swap(back_a.at[k, s], back_swapped_a.at[k, s], k, BACK_SWAP_A, s)
 
         def last():
             combine_b(k, me)

time: 101 us -> 101 us (level)
  no operation moved by 1% of the time
where the time goes in v10:
time: 101 us
  Pallas kernels  99.4 us (98%)
  local copies, waits for them, and re-layouts  1.32 us (1%)
    pallas_call x1, Pallas kernels, shards(): pl.pallas_call(functools.partial(kernel, n), out_shape=jax.ShapeDtypeStru...  99.4 us

profile of v10, /device:TPU:0, one launch (start us, length us, event | category | flops | bytes accessed | tf_op | source)
XLA Modules:
  0.0 100.7 jit_solution(16283250742901225058)
XLA Ops:
  0.0 99.4 %shard_map.55 = f32[1,128,4096]{2,1,0:T(8,128)S(1)} custom-call(f32[1,128,4096]{2,1,0:T(8,128)} %field.1, f32[1,1024,1024]{2,1,0:T(8,128)} %analysis.1, f32[1,1024,1024]{2,1,0:T(8,128)} %synthesis.1, f32[1,1024]{1,0:T(1,128)} %eigen_in.1, f32[1,512]{1,0:T(1,128)} %bitcast.1), custom_call_target="tpu_custom_call" | custom-call | tf_op jit(solution)/shard_map/pallas_call | solution.py:312
  99.4 1.3 %copy.7 = f32[1,128,4096]{2,1,0:T(8,128)} copy(f32[1,128,4096]{2,1,0:T(8,128)S(1)} %shard_map.55) | data formatting | bytes 4194304
